TPU v7x, 256 devices: a whole 4x4x8 slice. The times are simulated.
256 devices in a mesh: fsdp: 64 (over z, x, core), dp: 4 (over y).
Axes of the slice: x: 4, y: 4, z: 8, core: 2. Of those that a mesh axis runs over, the one named last changes fastest.
Arguments:
- grad: float32 [8192, 8192], P(('dp', 'fsdp')), parts along dimension 0, may hold values from -6 to 6
- moment: float32 [8192, 8192], P(('dp', 'fsdp')), parts along dimension 0, may hold values from -6 to 6
- second: float32 [8192, 8192], P('dp', 'fsdp'), parts along dimension 0, may hold values from 0.05 to 2
- left_basis: bfloat16 [8, 1024, 1024], P('dp', 'fsdp'), parts along dimension 0, may hold values from -0.1875 to 0.1875
- right_basis: bfloat16 [32, 1024, 1024], P('dp', 'fsdp'), parts along dimension 0, may hold values from -0.1875 to 0.1875
Outputs:
- update: float32 [8192, 8192], P(('dp', 'fsdp')), parts along dimension 0
- moment_new: float32 [8192, 8192], P(('dp', 'fsdp')), parts along dimension 0
- second_new: float32 [8192, 8192], P('dp', 'fsdp'), parts along dimension 0
There are 4 independent parts, one for each index of `dp`. A program takes and returns all parts, laid end to end along the dimension named above; each array names one. Nothing has to cross between parts.
All inputs are finite; a program needn't handle non-finite values.
Results may differ from a plain program's by a relative error of at most 0.0045.
Values may be sent and summed in bfloat16 or wider, within the bound.
A program may use at most 128 MiB of HBM per device.

v0:
```python
import jax
import jax.numpy as jnp
from jax import lax
from jax.sharding import PartitionSpec as P

BETA_ONE = 0.9
BETA_TWO = 0.95
EPSILON = 1e-08


def local(grad, moment, second, left_basis, right_basis):
    row_here = grad.shape[0]
    cols = grad.shape[1]
    width = left_basis.shape[2]
    lblocks = left_basis.shape[0]
    rblocks = right_basis.shape[0]
    col_here = second.shape[1]
    total_rows = second.shape[0]
    moment_new = BETA_ONE * moment + (1.0 - BETA_ONE) * grad
    packed = jnp.stack([grad, moment_new]).astype(jnp.bfloat16).reshape(2, row_here, rblocks, width)
    right_whole = lax.all_gather(right_basis, "fsdp", axis=1, tiled=True)
    turned = jnp.einsum("xrkb,kbi->xrki", packed, right_whole, preferred_element_type=jnp.float32)
    turned = turned.astype(jnp.bfloat16).reshape(2, row_here, cols)
    columns = lax.all_to_all(turned, "fsdp", split_axis=2, concat_axis=1, tiled=True)
    columns = columns.reshape(2, lblocks, width, col_here)
    projected = jnp.einsum(
        "xlkc,lki->xlic",
        columns,
        lax.all_gather(left_basis, "fsdp", axis=1, tiled=True),
        preferred_element_type=jnp.float32,
    )
    projected = projected.reshape(2, total_rows, col_here)
    grad_eigen = projected[0]
    moment_eigen = projected[1]
    second_new = BETA_TWO * second + (1.0 - BETA_TWO) * grad_eigen * grad_eigen
    scaled = (moment_eigen / (jnp.sqrt(second_new) + EPSILON)).astype(jnp.bfloat16)
    scaled = scaled.reshape(lblocks, width, col_here)
    back_left = jnp.einsum(
        "lki,lic->lkc",
        lax.all_gather(left_basis, "fsdp", axis=1, tiled=True),
        scaled,
        preferred_element_type=jnp.float32,
    )
    back_left = back_left.astype(jnp.bfloat16).reshape(total_rows, col_here)
    row_form = lax.all_to_all(back_left, "fsdp", split_axis=0, concat_axis=1, tiled=True)
    row_form = row_form.reshape(row_here, rblocks, width)
    update = jnp.einsum("rki,kbi->rkb", row_form, right_whole, preferred_element_type=jnp.float32)
    return (update.reshape(row_here, cols), moment_new, second_new)


def solution(mesh):
    in_specs = (
        P(("dp", "fsdp"), None),
        P(("dp", "fsdp"), None),
        P("dp", "fsdp"),
        P("dp", "fsdp", None),
        P("dp", "fsdp", None),
    )
    out_specs = (P(("dp", "fsdp"), None), P(("dp", "fsdp"), None), P("dp", "fsdp"))
    return jax.shard_map(local, mesh=mesh, in_specs=in_specs, out_specs=out_specs, check_vma=False)
```

profile of v0, /device:TPU:1, one launch (start us, length us, event | category | flops | bytes accessed | tf_op | source)
XLA Modules:
  0.0 248.3 jit_solution(5033446052847965112)
XLA Ops:
  7.2 0.0 all-gather.3.cloned.1.call-start
  7.2 0.7 all-gather.3.cloned.1.call-update
  7.9 0.0 all-gather.5.cloned.1.call-start
  7.9 0.7 all-gather.5.cloned.1.call-update
  8.6 3.0 %fusion.23 = (bf16[32,8192]{1,0:T(8,128)(2,1)S(1)}, f32[32,8192]{1,0:T(8,128)}, bf16[32,8192]{1,0:T(8,128)(2,1)S(1)}) fusion(f32[32,8192]{1,0:T(8,128)} %param.5, f32[32,8192]{1,0:T(8,128)} %param.6), kind=kLoop, calls=%fused_computation.21 | loop fusion | flops 1310720 | bytes 4194304 | tf_op jit(solution)/shard_map/convert.2
  11.7 0.3 copy.57
  12.0 0.3 copy.33
  12.3 0.3 copy.58
  12.6 0.3 copy.34
  12.9 101.8 %all-gather.3.cloned.1.call-done = bf16[8,1024,1024]{2,1,0:T(8,128)(2,1)} async-done(((bf16[8,16,1024]{2,1,0:T(8,128)(2,1)}), bf16[8,1024,1024]{2,1,0:T(8,128)(2,1)}) %all-gather.3.cloned.1.call-update) | async-done | bytes 16777232 | tf_op jit(solution)/shard_map/all_gather | solution.py:21
  114.7 8.8 %fusion.10 = bf16[2,32,8,1024]{3,1,0,2:T(8,128)(2,1)S(1)} fusion(bf16[8,1024,1024]{2,1,0:T(8,128)(2,1)} %all-gather.3.cloned.1.call-done, bf16[1,32,8,1024]{3,1,0,2:T(8,128)(2,1)S(1)} %copy.34, bf16[1,32,8,1024]{3,1,0,2:T(8,128)(2,1)S(1)} %copy.33), kind=kOutput, calls=%fused_computation.7 | convolution fusion | flops 1074790400 | bytes 18874368 | tf_op jit(solution)/shard_map/xrkb,kbi->xrki/dot_general | solution.py:22
  123.5 7.3 %copy.51 = bf16[2,32,8,1024]{1,0,3,2:T(2,128)(2,1)} copy(bf16[2,32,8,1024]{3,1,0,2:T(8,128)(2,1)S(1)} %fusion.10) | data formatting | bytes 2097152 | tf_op jit(solution)/shard_map/reshape | solution.py:23
  130.8 9.1 %reshape.47 = bf16[64,2,4096]{2,1,0:T(2,128)(2,1)S(1)} reshape(bf16[8192,2,32]{2,1,0:T(2,128)(2,1)} %bitcast.53) | data formatting | bytes 2097152
  140.0 35.8 %all_to_all.31 = bf16[64,2,4096]{2,1,0:T(2,128)(2,1)S(1)} all-to-all(bf16[64,2,4096]{2,1,0:T(2,128)(2,1)S(1)} %reshape.47), channel_id=1, replica_groups=mesh['fsdp'=64,'dp'=4] {'fsdp'}, dimensions={0} | all-to-all | bytes 2097152 | tf_op jit(solution)/shard_map/all_to_all | solution.py:24
  175.8 3.5 %reshape.48 = bf16[8192,2,32]{2,1,0:T(2,128)(2,1)} reshape(bf16[64,2,4096]{2,1,0:T(2,128)(2,1)S(1)} %all_to_all.31) | data formatting | bytes 2097152
  179.3 8.4 %copy.53 = bf16[2,32,64,128]{3,1,2,0:T(8,128)(2,1)S(1)} copy(bf16[2,32,64,128]{1,0,3,2:T(2,128)(2,1)} %bitcast.54) | data formatting | bytes 2097152 | tf_op jit(solution)/shard_map/all_to_all | solution.py:24
  187.7 7.3 %all-gather.5.cloned.1.call-done = bf16[2,1024,1024]{2,1,0:T(8,128)(2,1)} async-done(((bf16[2,16,1024]{2,1,0:T(8,128)(2,1)}), bf16[2,1024,1024]{2,1,0:T(8,128)(2,1)}) %all-gather.5.cloned.1.call-update) | async-done | bytes 4194320 | tf_op jit(solution)/shard_map/all_gather | solution.py:40
  194.9 3.5 %fusion.4 = f32[2,2,1024,128]{2,3,0,1:T(8,128)S(1)} fusion(bf16[2,1024,1024]{2,1,0:T(8,128)(2,1)} %all-gather.5.cloned.1.call-done, bf16[2,2,1024,128]{3,2,1,0:T(8,128)(2,1)S(1)} %bitcast.55), kind=kOutput, calls=%fused_computation.4 | convolution fusion | flops 1073741824 | bytes 7340032 | tf_op jit(solution)/shard_map/xlkc,lki->xlic/dot_general | solution.py:26
  198.4 0.1 fusion.24
  198.6 0.3 copy.40
  198.9 0.3 copy.41
  199.2 0.0 copy-start
  199.3 3.0 %fusion.18 = (bf16[2048,128]{1,0:T(8,128)(2,1)S(1)}, f32[2048,128]{1,0:T(8,128)}) fusion(f32[1,2,1024,128]{3,2,1,0:T(8,128)S(1)} %copy.40, f32[1,2,1024,128]{3,2,1,0:T(8,128)S(1)} %copy.41, f32[2048,128]{1,0:T(8,128)} %param.7), kind=kLoop, calls=%fused_computation.16 | loop fusion | flops 1835008 | bytes 4718592 | tf_op jit(solution)/shard_map/convert_element_type | solution.py:36
  202.2 0.0 copy-done
  202.2 1.5 fusion.13
  203.8 0.3 copy.43
  204.0 25.1 %all_to_all.32 = bf16[64,32,128]{2,1,0:T(8,128)(2,1)S(1)} all-to-all(bf16[64,32,128]{2,1,0:T(8,128)(2,1)S(1)} %bitcast.59), channel_id=1, replica_groups=mesh['fsdp'=64,'dp'=4] {'fsdp'}, dimensions={0} | all-to-all | bytes 1048576 | tf_op jit(solution)/shard_map/all_to_all | solution.py:45
  229.2 0.2 copy.44
  229.4 0.2 reshape.43
  229.6 10.8 %convolution_bitcast_fusion = f32[8,4,8,1024]{3,2,1,0:T(8,128)S(1)} fusion(bf16[8,1024,1024]{2,1,0:T(8,128)(2,1)} %all-gather.3.cloned.1.call-done, bf16[32,8,1024]{2,1,0:T(8,128)(2,1)S(1)} %reshape.43), kind=kOutput, calls=%fused_computation.8 | convolution fusion | flops 536870912 | bytes 18350080 | tf_op jit(solution)/shard_map/rki,kbi->rkb/dot_general | solution.py:47
  240.4 1.1 copy.56
Async XLA Ops:
  7.2 107.6 %all-gather.3.cloned.1.call-start = ((), (), s32[]{:S(2)}) async-start(), calls=%async_computation.2 | async-start | bytes 17039360 | tf_op jit(solution)/shard_map/all_gather | solution.py:21
  7.9 187.0 %all-gather.5.cloned.1.call-start = ((), (), s32[]{:S(2)}) async-start(), calls=%async_computation.3 | async-start | bytes 4259840 | tf_op jit(solution)/shard_map/all_gather | solution.py:40
  199.2 3.0 %copy-start = (bf16[2,1024,1024]{2,1,0:T(8,128)(2,1)S(1)}, bf16[2,1024,1024]{2,1,0:T(8,128)(2,1)}, u32[]{:S(2)}) copy-start(bf16[2,1024,1024]{2,1,0:T(8,128)(2,1)} %all-gather.5.cloned.1.call-done) | copy-start | bytes 12582916
Sparse Core Ops, SparseCore 0:
  10.8 103.8 all-gather.2
  117.5 77.3 all-gather.4
where the time goes:
time: 249 us; the launch traced here: 248 us
  waiting for transfers between devices  110 us (44%)
  blocking collectives  60.9 us (24%)
  local copies, waits for them, and re-layouts  32.1 us (13%)
  matrix products  24.6 us (10%)
  between operations  14.2 us (6%)
  other arithmetic  6.03 us (2%)
    all_gather x1, waiting for transfers between devices, local(): right_whole = lax.all_gather(right_basis, 'fsdp', axis=1, tiled=True)  102 us
    all_to_all x1, blocking collectives, local(): lax.all_to_all(turned, 'fsdp', split_axis=2, concat_axis=1, tiled=True)  35.8 us
    all_to_all x1, blocking collectives, local(): lax.all_to_all(back_left, 'fsdp', split_axis=0, concat_axis=1, tiled=True)  25.1 us
    unnamed x6, local copies, waits for them, and re-layouts  13.3 us
    dot_general x1, matrix products, local(): jnp.einsum('rki,kbi->rkb', row_form, right_whole, preferred_element_type=...  10.8 us
    dot_general x1, matrix products, local(): jnp.einsum('xrkb,kbi->xrki', packed, right_whole, preferred_element_type=...  8.79 us
    all_to_all x1, local copies, waits for them, and re-layouts, local(): lax.all_to_all(turned, 'fsdp', split_axis=2, concat_axis=1, tiled=True)  8.41 us
    reshape x1, local copies, waits for them, and re-layouts, local(): turned = turned.astype(jnp.bfloat16).reshape(2, row_here, cols)  7.3 us
  transfers between devices with their start and end apart: 2, of which 2 were waited for; matrix products, arithmetic and copies ran while one was open for 17% of the time, Pallas kernels for 0%

commit v1 on v0

v1 whole, which is shorter than its diff:
```python
import jax
import jax.numpy as jnp
from jax import lax
from jax.experimental import pallas as pl
from jax.experimental.pallas import tpu as pltpu
from jax.sharding import PartitionSpec as P

BETA_ONE = 0.9
BETA_TWO = 0.95
EPSILON = 1e-08

NZ, NX, NC = 8, 4, 2
NP = NX * NC
F32, BF16 = jnp.float32, jnp.bfloat16


def kernel(
    grad, moment, second, left, right,
    upd_o, mom_o, sec_o,
    gv, mv, sv, ps, pr, rb, tb, cb, lb, sc, bk, wb, ub,
    in_sem, out_sem,
    rz_s, rz_r, rx_s, rx_r, rd_s, rd_r,
    lz_s, lz_r, lx_s, lx_r, lo_s, lo_r, ld_s, ld_r,
    pz_s, pz_r, tx_s, tx_r, bx_s, bx_r, uz_s, uz_r,
):
    f = lax.axis_index("fsdp")
    z, p = f // NP, lax.rem(f, NP)
    x, c = p // NC, lax.rem(p, NC)
    row = gv.shape[0]
    width = rb.shape[-1]

    def dev(zz, xx, cc):
        return {"fsdp": (zz * NX + xx) * NC + cc}

    def up(v, d, n):
        return lax.rem(v + d + 2 * n, n)

    def zdev(d):
        return dev(up(z, d, NZ), x, c)

    def xdev(d):
        return dev(z, up(x, d, NX), c)

    other = dev(z, x, 1 - c)

    def remote(src, dst, ss, rs, to):
        return pltpu.make_async_remote_copy(
            src_ref=src, dst_ref=dst, send_sem=ss, recv_sem=rs, device_id=to, device_id_type=pl.DeviceIdType.MESH
        )

    def wait(ref, sem):
        pltpu.make_async_copy(ref, ref, sem).wait()

    loads = [
        pltpu.make_async_copy(grad, gv, in_sem.at[0]),
        pltpu.make_async_copy(moment, mv, in_sem.at[1]),
        pltpu.make_async_copy(second, sv, in_sem.at[2]),
        pltpu.make_async_copy(left, lb.at[:, z, x, c], in_sem.at[3]),
        pltpu.make_async_copy(right.at[z], rb.at[z, x, c], in_sem.at[4]),
    ]
    for load in loads:
        load.start()

    barrier = pltpu.get_barrier_semaphore()

    def greet(d, carry):
        pl.semaphore_signal(barrier, inc=1, device_id=zdev(d), device_id_type=pl.DeviceIdType.MESH)
        pl.semaphore_signal(
            barrier, inc=1, device_id={"fsdp": z * NP + lax.rem(p + d, NP)}, device_id_type=pl.DeviceIdType.MESH
        )
        return carry

    lax.fori_loop(1, NZ, greet, 0)

    loads[0].wait()
    loads[1].wait()

    def pack(k, carry):
        cols = pl.ds(pl.multiple_of(k * width, width), width)
        g = gv[:, cols]
        m = BETA_ONE * mv[:, cols] + (1.0 - BETA_ONE) * g
        mv[:, cols] = m
        ps[k, 0:row] = g.astype(BF16)
        ps[k, row : 2 * row] = m.astype(BF16)
        return carry

    lax.fori_loop(0, NZ, pack, 0)
    store_m = pltpu.make_async_copy(mv, mom_o, out_sem.at[0])
    store_m.start()
    pr[z] = ps[z]
    loads[3].wait()
    loads[4].wait()

    pl.semaphore_wait(barrier, 2 * (NZ - 1))

    def right_z(d, carry):
        k = up(z, d, NZ)
        remote(right.at[k], rb.at[z, x, c], rz_s, rz_r, zdev(d)).start()
        return carry

    lax.fori_loop(1, NZ, right_z, 0)

    def left_z(s, way, half=False):
        sign = 1 if way == 0 else -1
        blk = up(z, -sign * (s - 1), NZ)
        if half:
            ref = lb.at[way, blk, x, c]
        else:
            ref = lb.at[:, blk, x, c]
        return remote(ref, ref, lz_s.at[s, way], lz_r.at[s, way], zdev(sign))

    for way in range(2):
        left_z(1, way).start()

    def packed_z(i, carry):
        d = (i + 2) // 2
        off = jnp.where(lax.rem(i, 2) == 0, d, -d)
        k = up(z, off, NZ)
        remote(ps.at[k], pr.at[z], pz_s, pz_r.at[z], dev(k, x, c)).start()
        return carry

    lax.fori_loop(0, NZ - 1, packed_z, 0)

    def right_x(way):
        ref = rb.at[:, x, c]
        return remote(ref, ref, rx_s.at[way], rx_r.at[way], xdev(1 if way == 0 else -1))

    def right_half(way):
        ref = rb.at[pl.ds(way * (NZ // 2), NZ // 2), up(x, -1 if way == 0 else 1, NX), c]
        return remote(ref, ref, rx_s.at[2 + way], rx_r.at[2 + way], xdev(1 if way == 0 else -1))

    def right_core(xx, i):
        ref = rb.at[:, xx, c]
        return remote(ref, ref, rd_s.at[i], rd_r.at[i], other)

    def left_x(zz, way):
        ref = lb.at[:, zz, x, c]
        return remote(ref, ref, lx_s.at[zz, way], lx_r.at[zz, way], xdev(1 if way == 0 else -1))

    def left_half(zz, way):
        ref = lb.at[way, zz, up(x, -1 if way == 0 else 1, NX), c]
        return remote(ref, ref, lo_s.at[zz, way], lo_r.at[zz, way], xdev(1 if way == 0 else -1))

    def left_core(zz):
        ref = lb.at[:, zz, :, c]
        return remote(ref, ref, ld_s.at[zz], ld_r.at[zz], other)

    def blocks(s):
        if s == 0 or s == NZ // 2:
            return [up(z, s, NZ)]
        return [up(z, -s, NZ), up(z, s, NZ)]

    def stage(s):
        if 1 <= s <= NZ // 2:
            for way in range(2):
                left_z(s, way, half=s == NZ // 2).wait_recv()
                if s < NZ // 2:
                    left_z(s + 1, way, half=s + 1 == NZ // 2).start()
        if s <= NZ // 2:
            for zz in blocks(s):
                for way in range(2):
                    left_x(zz, way).start()
        if 1 <= s <= NZ // 2 + 1:
            for zz in blocks(s - 1):
                for way in range(2):
                    left_x(zz, way).wait_recv()
                    left_half(zz, way).start()
        if 2 <= s <= NZ // 2 + 2:
            for zz in blocks(s - 2):
                for way in range(2):
                    left_half(zz, way).wait_recv()
                left_core(zz).start()

    wait(right.at[pl.ds(0, NZ - 1)], rz_r)
    for way in range(2):
        right_x(way).start()
    right_core(x, 0).start()
    stage(0)
    for way in range(2):
        right_x(way).wait_recv()
        right_half(way).start()
        right_core(up(x, -1 if way == 0 else 1, NX), 1 + way).start()
    stage(1)
    for way in range(2):
        right_half(way).wait_recv()
    right_core(up(x, 2, NX), 3).start()
    stage(2)
    for i in range(4):
        right_core(x, i).wait_recv()

    def turn(i, carry):
        d = (i + 1) // 2
        zz = up(z, jnp.where(lax.rem(i, 2) == 1, -d, d), NZ)

        @pl.when(i > 0)
        def _():
            wait(pr.at[zz], pz_r.at[zz])

        t = jnp.dot(pr[zz], rb[...].reshape(width, width), preferred_element_type=F32).astype(BF16)
        seg = width // NP
        for q in range(NP):
            tb[zz, q, :, 0:seg] = t[0:row, q * seg : (q + 1) * seg]
            tb[zz, q, :, seg : 2 * seg] = t[row : 2 * row, q * seg : (q + 1) * seg]
        cb[zz, p] = tb[zz, p]

        def send(e, carry):
            q = lax.rem(p + e, NP)
            remote(tb.at[zz, q], cb.at[zz, p], tx_s, tx_r, {"fsdp": z * NP + q}).start()
            return carry

        lax.fori_loop(1, NP, send, 0)
        return carry

    lax.fori_loop(0, 3, turn, 0)
    stage(3)
    lax.fori_loop(3, 5, turn, 0)
    stage(4)
    lax.fori_loop(5, 7, turn, 0)
    stage(5)
    lax.fori_loop(7, 8, turn, 0)
    stage(6)

    def left_done(zz, carry):
        left_core(zz).wait_recv()
        return carry

    lax.fori_loop(0, NZ, left_done, 0)
    wait(cb.at[pl.ds(0, NZ - 1)], tx_r)
    loads[2].wait()

    seg = width // NP
    part = width // 4

    def project(i, carry):
        l, q = i // 4, lax.rem(i, 4)
        cols = pl.ds(pl.multiple_of(q * part, part), part)
        basis = lb[l, :, :, :, :, cols].reshape(width, part)
        turned = cb[pl.ds(l * (NZ // 2), NZ // 2)].reshape(width, 2 * seg)
        both = lax.dot_general(basis, turned, (((0,), (0,)), ((), ())), preferred_element_type=F32)
        g, m = both[:, :seg], both[:, seg:]
        rows = pl.ds(pl.multiple_of(i * part, part), part)
        s = BETA_TWO * sv[rows, :] + (1.0 - BETA_TWO) * g * g
        sv[rows, :] = s
        sc[rows, :] = (m / (jnp.sqrt(s) + EPSILON)).astype(BF16)
        return carry

    lax.fori_loop(0, 8, project, 0)
    store_s = pltpu.make_async_copy(sv, sec_o, out_sem.at[1])
    store_s.start()

    def far(i):
        d = (NZ - i) // 2
        return up(z, jnp.where(lax.rem(i, 2) == 1, d, -d), NZ)

    def back(i, carry):
        zz = far(i)
        l, q = zz // 4, lax.rem(zz, 4)
        basis = lb[l, pl.ds(2 * q, 2)].reshape(NP * row, width)
        scaled = sc[pl.ds(pl.multiple_of(l * width, width), width), :]
        out = jnp.dot(basis, scaled, preferred_element_type=F32).astype(BF16)
        bk[zz] = out.reshape(NP, row, seg)
        wb[zz, p] = bk[zz, p]

        def send(e, carry):
            q = lax.rem(p + e, NP)
            remote(bk.at[zz, q], wb.at[zz, p], bx_s, bx_r.at[zz], {"fsdp": z * NP + q}).start()
            return carry

        lax.fori_loop(1, NP, send, 0)
        return carry

    lax.fori_loop(0, NZ, back, 0)

    mine = pl.ds(pl.multiple_of(z * width, width), width)

    def update(i, carry):
        zz = far(i)
        wait(wb.at[zz, pl.ds(0, NP - 1)], bx_r.at[zz])
        rows = jnp.concatenate([wb[zz, q] for q in range(NP)], axis=1)
        out = lax.dot_general(
            rows, rb[...].reshape(width, width), (((1,), (1,)), ((), ())), preferred_element_type=F32
        )
        ub[zz] = out.astype(BF16)

        @pl.when(i < NZ - 1)
        def _():
            remote(ub.at[zz], upd_o.at[:, mine], uz_s, uz_r, dev(zz, x, c)).start()

        return carry

    lax.fori_loop(0, NZ, update, 0)
    store_u = pltpu.make_async_copy(ub.at[z], upd_o.at[:, mine], out_sem.at[2])
    store_u.start()

    for way in range(2):
        right_x(way).wait_send()
        right_half(way).wait_send()
        for s in range(1, NZ // 2 + 1):
            left_z(s, way, half=s == NZ // 2).wait_send()
    for i in range(4):
        right_core(x, i).wait_send()

    def drain(zz, carry):
        for way in range(2):
            left_x(zz, way).wait_send()
            left_half(zz, way).wait_send()
        left_core(zz).wait_send()
        return carry

    lax.fori_loop(0, NZ, drain, 0)
    wait(right.at[pl.ds(0, NZ - 1)], rz_s)
    wait(ps.at[pl.ds(0, NZ - 1)], pz_s)
    wait(tb.at[pl.ds(0, NZ - 1)], tx_s)
    wait(bk.at[pl.ds(0, NZ - 1)], bx_s)
    wait(ub.at[pl.ds(0, NZ - 1)], uz_s)
    wait(ub.at[pl.ds(0, NZ - 1)], uz_r)
    store_m.wait()
    store_s.wait()
    store_u.wait()


def local(grad, moment, second, left_basis, right_basis):
    row, cols = grad.shape
    lblocks, piece, width = left_basis.shape
    total, seg = second.shape
    any_spec = pl.BlockSpec(memory_space=pl.ANY)
    dma = pltpu.SemaphoreType.DMA
    update, moment_new, second_new = pl.pallas_call(
        kernel,
        out_shape=(
            jax.ShapeDtypeStruct((row, cols), BF16),
            jax.ShapeDtypeStruct((row, cols), F32),
            jax.ShapeDtypeStruct((total, seg), F32),
        ),
        in_specs=[any_spec] * 5,
        out_specs=[any_spec] * 3,
        scratch_shapes=[
            pltpu.VMEM((row, cols), F32),
            pltpu.VMEM((row, cols), F32),
            pltpu.VMEM((total, seg), F32),
            pltpu.VMEM((NZ, 2 * row, width), BF16),
            pltpu.VMEM((NZ, 2 * row, width), BF16),
            pltpu.VMEM((NZ, NX, NC, piece, width), BF16),
            pltpu.VMEM((NZ, NP, row, 2 * seg), BF16),
            pltpu.VMEM((NZ, NP, row, 2 * seg), BF16),
            pltpu.VMEM((lblocks, NZ, NX, NC, piece, width), BF16),
            pltpu.VMEM((total, seg), BF16),
            pltpu.VMEM((NZ, NP, row, seg), BF16),
            pltpu.VMEM((NZ, NP, row, seg), BF16),
            pltpu.VMEM((NZ, row, width), BF16),
            dma((5,)), dma((3,)),
            dma, dma, dma((4,)), dma((4,)), dma((4,)), dma((4,)),
            dma((5, 2)), dma((5, 2)), dma((NZ, 2)), dma((NZ, 2)), dma((NZ, 2)), dma((NZ, 2)), dma((NZ,)), dma((NZ,)),
            dma, dma((NZ,)), dma, dma, dma, dma((NZ,)), dma, dma,
        ],
        compiler_params=pltpu.CompilerParams(
            collective_id=0, has_side_effects=True, vmem_limit_bytes=40 * 2**20
        ),
        cost_estimate=pl.CostEstimate(flops=3 * 2**30, bytes_accessed=8 * 2**20, transcendentals=2**19),
        name="soap_step",
    )(grad, moment, second, left_basis, right_basis)
    return update.astype(F32), moment_new, second_new


def solution(mesh):
    in_specs = (
        P(("dp", "fsdp"), None),
        P(("dp", "fsdp"), None),
        P("dp", "fsdp"),
        P("dp", "fsdp", None),
        P("dp", "fsdp", None),
    )
    out_specs = (P(("dp", "fsdp"), None), P(("dp", "fsdp"), None), P("dp", "fsdp"))
    return jax.shard_map(local, mesh=mesh, in_specs=in_specs, out_specs=out_specs, check_vma=False)
```

time: 249 us -> 102 us (0.41)
  waiting for transfers between devices: 110 us -> 0 us
  Pallas kernels: 0 us -> 92.7 us
  blocking collectives: 60.9 us -> 0 us
  local copies, waits for them, and re-layouts: 32.1 us -> 7.39 us
  matrix products: 24.6 us -> 0 us
  between operations: 14.2 us -> 0.65 us
  other arithmetic: 6.03 us -> 1.04 us
    all_gather x2 -> x0, waiting for transfers between devices: 109 us -> none  [the longest x1 102 us: local(): right_whole = lax.all_gather(right_basis, 'fsdp', axis=1, tiled=True)]
    pallas_call x0 -> x1, Pallas kernels: none -> 92.7 us  [local(): pl.pallas_call(kernel, out_shape=(jax.ShapeDtypeStruct((row, cols), BF16)...]
    all_to_all x2 -> x0, blocking collectives: 60.9 us -> none  [the longest x1 35.8 us: local(): lax.all_to_all(turned, 'fsdp', split_axis=2, concat_axis=1, tiled=True)]
    dot_general x4 -> x0, matrix products: 24.6 us -> none  [the longest x1 10.8 us: local(): jnp.einsum('rki,kbi->rkb', row_form, right_whole, preferred_element_type=...]
    all_to_all x2 -> x0, local copies, waits for them, and re-layouts: 8.61 us -> none  [the longest x1 8.41 us: local(): lax.all_to_all(turned, 'fsdp', split_axis=2, concat_axis=1, tiled=True)]
    reshape x3 -> x0, local copies, waits for them, and re-layouts: 8.58 us -> none  [the longest x1 7.3 us: local(): turned = turned.astype(jnp.bfloat16).reshape(2, row_here, cols)]
    unnamed x6 -> x12, local copies, waits for them, and re-layouts: 13.3 us -> 7.39 us
    another operation x1 -> x0, other arithmetic: 3.04 us -> none
  transfers between devices with their start and end apart: 2 -> 0, of which waited for: 2 -> 0; matrix products, arithmetic and copies ran while one was open for 17% -> 0% of each run, Pallas kernels for 0% -> 0%
where the time goes in v1:
time: 102 us
  Pallas kernels  92.7 us (91%)
  local copies, waits for them, and re-layouts  7.39 us (7%)
  other arithmetic  1.04 us (1%)
    pallas_call x1, Pallas kernels, local(): pl.pallas_call(kernel, out_shape=(jax.ShapeDtypeStruct((row, cols), BF16)...  92.7 us
    unnamed x12, local copies, waits for them, and re-layouts  7.39 us

profile of v1, /device:TPU:1, one launch (start us, length us, event | category | flops | bytes accessed | tf_op | source)
XLA Modules:
  0.0 101.8 jit_solution(2395030393714469004)
XLA Ops:
  0.6 0.0 copy-start
  0.6 1.2 %copy-done = f32[32,8192]{1,0:T(8,128)S(1)} copy-done((f32[32,8192]{1,0:T(8,128)S(1)}, f32[32,8192]{1,0:T(8,128)}, u32[]{:S(2)}) %copy-start) | copy-done | bytes 1048600
  1.9 0.0 copy-start.1
  1.9 1.2 %copy-done.1 = f32[32,8192]{1,0:T(8,128)S(1)} copy-done((f32[32,8192]{1,0:T(8,128)S(1)}, f32[32,8192]{1,0:T(8,128)}, u32[]{:S(2)}) %copy-start.1) | copy-done | bytes 1048600
  3.1 0.0 copy-start.2
  3.1 1.2 %copy-done.2 = f32[2048,128]{1,0:T(8,128)S(1)} copy-done((f32[2048,128]{1,0:T(8,128)S(1)}, f32[2048,128]{1,0:T(8,128)}, u32[]{:S(2)}) %copy-start.2) | copy-done | bytes 1048600
  4.3 0.0 copy-start.3
  4.3 0.9 copy-done.3
  5.3 0.0 copy-start.4
  5.3 0.8 copy-done.4
  6.1 92.7 %soap_step.1 = (bf16[32,8192]{1,0:T(8,128)(2,1)S(1)}, f32[32,8192]{1,0:T(8,128)S(1)}, f32[2048,128]{1,0:T(8,128)S(1)}) custom-call(f32[32,8192]{1,0:T(8,128)S(1)} %copy-done, f32[32,8192]{1,0:T(8,128)S(1)} %copy-done.1, f32[2048,128]{1,0:T(8,128)S(1)} %copy-done.2, bf16[2,16,1024]{2,1,0:T(8,128)(2,1)S(1)} %copy-done.4, bf16[8,16,1024]{2,1,0:T(8,128)(2,1)S(1)} %copy-done.3), custom_call_target="tpu_custom_call" | custom-call | flops 3221225472 | bytes 8388608 | tf_op jit(solution)/shard_map/soap_step/pallas_call | solution.py:328
  98.8 1.0 %convert_element_type.3 = f32[32,8192]{1,0:T(8,128)} convert(bf16[32,8192]{1,0:T(8,128)(2,1)S(1)} %get-tuple-element.6) | non-fusion elementwise | flops 262144 | bytes 1572864 | tf_op jit(solution)/shard_map/convert_element_type | solution.py:362
  99.9 1.0 copy.10
  100.8 1.0 copy.11
Async XLA Ops:
  0.6 1.2 %copy-start = (f32[32,8192]{1,0:T(8,128)S(1)}, f32[32,8192]{1,0:T(8,128)}, u32[]{:S(2)}) copy-start(f32[32,8192]{1,0:T(8,128)} %grad.1) | copy-start | bytes 3145732
  1.9 1.2 %copy-start.1 = (f32[32,8192]{1,0:T(8,128)S(1)}, f32[32,8192]{1,0:T(8,128)}, u32[]{:S(2)}) copy-start(f32[32,8192]{1,0:T(8,128)} %moment.1) | copy-start | bytes 3145732
  3.1 1.2 %copy-start.2 = (f32[2048,128]{1,0:T(8,128)S(1)}, f32[2048,128]{1,0:T(8,128)}, u32[]{:S(2)}) copy-start(f32[2048,128]{1,0:T(8,128)} %second.1) | copy-start | bytes 3145732
  4.3 0.9 copy-start.3
  5.3 0.8 copy-start.4

commit v2 on v1

--- a/solution.py
+++ b/solution.py
@@ -98,28 +98,15 @@
         remote(right.at[k], rb.at[z, x, c], rz_s, rz_r, zdev(d)).start()
         return carry
 
-    lax.fori_loop(1, NZ, right_z, 0)
-
-    def left_z(s, way, half=False):
+    def left_z(step, way):
         sign = 1 if way == 0 else -1
-        blk = up(z, -sign * (s - 1), NZ)
-        if half:
-            ref = lb.at[way, blk, x, c]
-        else:
-            ref = lb.at[:, blk, x, c]
-        return remote(ref, ref, lz_s.at[s, way], lz_r.at[s, way], zdev(sign))
-
-    for way in range(2):
-        left_z(1, way).start()
-
-    def packed_z(i, carry):
-        d = (i + 2) // 2
-        off = jnp.where(lax.rem(i, 2) == 0, d, -d)
-        k = up(z, off, NZ)
+        blk = z if step < 2 else up(z, -2 * sign, NZ)
+        ref = lb.at[way, blk, x, c] if step == 3 else lb.at[:, blk, x, c]
+        return remote(ref, ref, lz_s.at[step, way], lz_r.at[step, way], zdev((1, 2, 1, 2)[step] * sign))
+
+    def packed_z(d):
+        k = up(z, d, NZ)
         remote(ps.at[k], pr.at[z], pz_s, pz_r.at[z], dev(k, x, c)).start()
-        return carry
-
-    lax.fori_loop(0, NZ - 1, packed_z, 0)
 
     def right_x(way):
         ref = rb.at[:, x, c]
@@ -145,52 +132,81 @@
         ref = lb.at[:, zz, :, c]
         return remote(ref, ref, ld_s.at[zz], ld_r.at[zz], other)
 
-    def blocks(s):
-        if s == 0 or s == NZ // 2:
-            return [up(z, s, NZ)]
-        return [up(z, -s, NZ), up(z, s, NZ)]
-
-    def stage(s):
-        if 1 <= s <= NZ // 2:
+    def near(d):
+        return [up(z, -d, NZ), up(z, d, NZ)]
+
+    def left_send(group):
+        for zz in group:
             for way in range(2):
-                left_z(s, way, half=s == NZ // 2).wait_recv()
-                if s < NZ // 2:
-                    left_z(s + 1, way, half=s + 1 == NZ // 2).start()
-        if s <= NZ // 2:
-            for zz in blocks(s):
-                for way in range(2):
-                    left_x(zz, way).start()
-        if 1 <= s <= NZ // 2 + 1:
-            for zz in blocks(s - 1):
-                for way in range(2):
-                    left_x(zz, way).wait_recv()
-                    left_half(zz, way).start()
-        if 2 <= s <= NZ // 2 + 2:
-            for zz in blocks(s - 2):
-                for way in range(2):
-                    left_half(zz, way).wait_recv()
-                left_core(zz).start()
+                left_x(zz, way).start()
+
+    def left_pass(group):
+        for zz in group:
+            for way in range(2):
+                left_x(zz, way).wait_recv()
+                left_half(zz, way).start()
+
+    def left_share(group):
+        for zz in group:
+            for way in range(2):
+                left_half(zz, way).wait_recv()
+            left_core(zz).start()
+
+    own, two, last = [z], near(2), near(3) + [up(z, 4, NZ)]
+
+    for way in range(2):
+        left_z(0, way).start()
+    left_send(own)
+    lax.fori_loop(1, NZ, right_z, 0)
+    for way in range(2):
+        left_z(1, way).start()
+    packed_z(1)
+    packed_z(-1)
+
+    for way in range(2):
+        left_z(0, way).wait_recv()
+    left_send(near(1))
+    left_pass(own)
 
     wait(right.at[pl.ds(0, NZ - 1)], rz_r)
     for way in range(2):
         right_x(way).start()
     right_core(x, 0).start()
-    stage(0)
+
+    for way in range(2):
+        left_z(1, way).wait_recv()
+        left_z(2, way).start()
+        left_z(3, way).start()
+    packed_z(3)
+    packed_z(-3)
+    left_send(two)
+    left_pass(near(1))
+    left_share(own)
+
     for way in range(2):
         right_x(way).wait_recv()
         right_half(way).start()
         right_core(up(x, -1 if way == 0 else 1, NX), 1 + way).start()
-    stage(1)
+
+    for way in range(2):
+        left_z(2, way).wait_recv()
+        left_z(3, way).wait_recv()
+    for d in (4, 2, -2):
+        packed_z(d)
+    left_send(last)
+    left_pass(two)
+    left_share(near(1))
+
     for way in range(2):
         right_half(way).wait_recv()
     right_core(up(x, 2, NX), 3).start()
-    stage(2)
     for i in range(4):
         right_core(x, i).wait_recv()
 
     def turn(i, carry):
-        d = (i + 1) // 2
-        zz = up(z, jnp.where(lax.rem(i, 2) == 1, -d, d), NZ)
+        d = jnp.where(i < 3, (i + 1) // 2, jnp.where(i < 5, 3, jnp.where(i == 5, 4, 2)))
+        odd = jnp.where(i > 5, lax.rem(i + 1, 2), lax.rem(i, 2))
+        zz = up(z, jnp.where(odd == 1, -d, d), NZ)
 
         @pl.when(i > 0)
         def _():
@@ -212,13 +228,11 @@
         return carry
 
     lax.fori_loop(0, 3, turn, 0)
-    stage(3)
+    left_pass(last)
+    left_share(two)
     lax.fori_loop(3, 5, turn, 0)
-    stage(4)
-    lax.fori_loop(5, 7, turn, 0)
-    stage(5)
-    lax.fori_loop(7, 8, turn, 0)
-    stage(6)
+    left_share(last)
+    lax.fori_loop(5, 8, turn, 0)
 
     def left_done(zz, carry):
         left_core(zz).wait_recv()
@@ -295,8 +309,8 @@
     for way in range(2):
         right_x(way).wait_send()
         right_half(way).wait_send()
-        for s in range(1, NZ // 2 + 1):
-            left_z(s, way, half=s == NZ // 2).wait_send()
+        for step in range(4):
+            left_z(step, way).wait_send()
     for i in range(4):
         right_core(x, i).wait_send()
 
@@ -350,11 +364,11 @@
             pltpu.VMEM((NZ, row, width), BF16),
             dma((5,)), dma((3,)),
             dma, dma, dma((4,)), dma((4,)), dma((4,)), dma((4,)),
-            dma((5, 2)), dma((5, 2)), dma((NZ, 2)), dma((NZ, 2)), dma((NZ, 2)), dma((NZ, 2)), dma((NZ,)), dma((NZ,)),
+            dma((4, 2)), dma((4, 2)), dma((NZ, 2)), dma((NZ, 2)), dma((NZ, 2)), dma((NZ, 2)), dma((NZ,)), dma((NZ,)),
             dma, dma((NZ,)), dma, dma, dma, dma((NZ,)), dma, dma,
         ],
         compiler_params=pltpu.CompilerParams(
-            collective_id=0, has_side_effects=True, vmem_limit_bytes=40 * 2**20
+            collective_id=0, has_side_effects=True, vmem_limit_bytes=62 * 2**20
         ),
         cost_estimate=pl.CostEstimate(flops=3 * 2**30, bytes_accessed=8 * 2**20, transcendentals=2**19),
         name="soap_step",

time: 102 us -> 82.4 us (0.81)
  Pallas kernels: 92.7 us -> 76.8 us
  local copies, waits for them, and re-layouts: 7.39 us -> 2.58 us
  other arithmetic: 1.04 us -> 2.17 us
    pallas_call x1, Pallas kernels: 92.7 us -> 76.8 us  [local(): pl.pallas_call(kernel, out_shape=(jax.ShapeDtypeStruct((row, cols), BF16)...]
    unnamed x12 -> x6, local copies, waits for them, and re-layouts: 7.39 us -> 2.58 us
    convert_element_type x1, other arithmetic: 1.04 us -> 2.17 us  [local(): return (update.astype(F32), moment_new, second_new)]
where the time goes in v2:
time: 82.4 us; the launch traced here: 82.2 us
  Pallas kernels  76.8 us (93%)
  local copies, waits for them, and re-layouts  2.58 us (3%)
  other arithmetic  2.17 us (3%)
    pallas_call x1, Pallas kernels, local(): pl.pallas_call(kernel, out_shape=(jax.ShapeDtypeStruct((row, cols), BF16)...  76.8 us
    unnamed x6, local copies, waits for them, and re-layouts  2.58 us
    convert_element_type x1, other arithmetic, local(): return (update.astype(F32), moment_new, second_new)  2.17 us

profile of v2, /device:TPU:1, one launch (start us, length us, event | category | flops | bytes accessed | tf_op | source)
XLA Modules:
  0.0 82.2 jit_solution(15024728375916630165)
XLA Ops:
  0.6 76.8 %soap_step.1 = (bf16[32,8192]{1,0:T(8,128)(2,1)}, f32[32,8192]{1,0:T(8,128)}, f32[2048,128]{1,0:T(8,128)}) custom-call(f32[32,8192]{1,0:T(8,128)} %grad.1, f32[32,8192]{1,0:T(8,128)} %moment.1, f32[2048,128]{1,0:T(8,128)} %second.1, bf16[2,16,1024]{2,1,0:T(8,128)(2,1)} %left.1, bf16[8,16,1024]{2,1,0:T(8,128)(2,1)} %right.1), custom_call_target="tpu_custom_call" | custom-call | flops 3221225472 | bytes 8388608 | tf_op jit(solution)/shard_map/soap_step/pallas_call | solution.py:342
  77.4 0.0 copy-start.1
  77.5 2.2 %convert_element_type.3 = f32[32,8192]{1,0:T(8,128)} convert(bf16[32,8192]{1,0:T(8,128)(2,1)} %get-tuple-element.6) | non-fusion elementwise | flops 262144 | bytes 1572864 | tf_op jit(solution)/shard_map/convert_element_type | solution.py:376
  79.6 0.0 copy-done.1
  79.6 0.0 copy-start
  79.6 1.0 %copy.10 = f32[32,8192]{1,0:T(8,128)} copy(f32[32,8192]{1,0:T(8,128)S(1)} %copy-done.1) | data formatting | bytes 2097152
  80.6 0.6 copy-done
  81.2 1.0 %copy.11 = f32[2048,128]{1,0:T(8,128)} copy(f32[2048,128]{1,0:T(8,128)S(1)} %copy-done) | data formatting | bytes 2097152
Async XLA Ops:
  77.4 2.2 %copy-start.1 = (f32[32,8192]{1,0:T(8,128)S(1)}, f32[32,8192]{1,0:T(8,128)}, u32[]{:S(2)}) copy-start(f32[32,8192]{1,0:T(8,128)} %get-tuple-element.13) | copy-start | bytes 3145732
  79.6 1.6 %copy-start = (f32[2048,128]{1,0:T(8,128)S(1)}, f32[2048,128]{1,0:T(8,128)}, u32[]{:S(2)}) copy-start(f32[2048,128]{1,0:T(8,128)} %get-tuple-element.14) | copy-start | bytes 3145732

commit v3 on v2

v3 whole, which is shorter than its diff:
```python
import jax
import jax.numpy as jnp
from jax import lax
from jax.experimental import pallas as pl
from jax.experimental.pallas import tpu as pltpu
from jax.sharding import PartitionSpec as P

BETA_ONE = 0.9
BETA_TWO = 0.95
EPSILON = 1e-08

NZ, NX, NC = 8, 4, 2
NP = NX * NC
F32, BF16 = jnp.float32, jnp.bfloat16

FILL = (1, -1)
REST = (2, -2, 3, -3, 4)


def kernel(
    grad, moment, second, left, right,
    upd_o, mom_o, sec_o,
    gv, mv, sv, ps, pr, rb, tb, cb, lb, ac, sc, bk, wb, ub,
    in_sem, out_sem,
    rz_s, rz_r, rx_s, rx_r, rd_s, rd_r,
    lz_s, lz_r, lx_s, lx_r, lo_s, lo_r, ld_s, ld_r,
    pz_s, pz_r, tx_s, tx_r, bx_s, bx_r, uz_s, uz_r,
):
    f = lax.axis_index("fsdp")
    z, p = f // NP, lax.rem(f, NP)
    x, c = p // NC, lax.rem(p, NC)
    row = gv.shape[0]
    width = rb.shape[-1]

    def dev(zz, xx, cc):
        return {"fsdp": (zz * NX + xx) * NC + cc}

    def up(v, d, n):
        return lax.rem(v + d + 2 * n, n)

    def zdev(d):
        return dev(up(z, d, NZ), x, c)

    def xdev(d):
        return dev(z, up(x, d, NX), c)

    other = dev(z, x, 1 - c)

    def remote(src, dst, ss, rs, to):
        return pltpu.make_async_remote_copy(
            src_ref=src, dst_ref=dst, send_sem=ss, recv_sem=rs, device_id=to, device_id_type=pl.DeviceIdType.MESH
        )

    def wait(ref, sem):
        pltpu.make_async_copy(ref, ref, sem).wait()

    barrier = pltpu.get_barrier_semaphore()
    for d in (4, 3, -3, 2, -2, 1, -1):
        pl.semaphore_signal(barrier, inc=1, device_id=zdev(d), device_id_type=pl.DeviceIdType.MESH)
    for d in range(1, NP):
        to = {"fsdp": z * NP + lax.rem(p + d, NP)}
        pl.semaphore_signal(barrier, inc=1, device_id=to, device_id_type=pl.DeviceIdType.MESH)

    loads = [
        pltpu.make_async_copy(left, lb.at[:, z, x, c], in_sem.at[0]),
        pltpu.make_async_copy(right.at[z], rb.at[z, x, c], in_sem.at[1]),
        pltpu.make_async_copy(grad, gv, in_sem.at[2]),
        pltpu.make_async_copy(moment, mv, in_sem.at[3]),
        pltpu.make_async_copy(second, sv, in_sem.at[4]),
    ]
    for load in loads:
        load.start()
    ac[...] = jnp.zeros_like(ac)
    loads[0].wait()
    loads[1].wait()
    pl.semaphore_wait(barrier, 2 * (NZ - 1))

    def right_z(d):
        group = 0 if abs(d) <= 2 else 1
        remote(right.at[up(z, d, NZ)], rb.at[z, x, c], rz_s, rz_r.at[group], zdev(d)).start()

    def left_z(step, way):
        sign = 1 if way == 0 else -1
        blk = up(z, -(0, 1, 2, 2)[step] * sign, NZ)
        ref = lb.at[way, blk, x, c] if step == 3 else lb.at[:, blk, x, c]
        return remote(ref, ref, lz_s.at[step, way], lz_r.at[step, way], zdev((1, 1, 1, 2)[step] * sign))

    def packed_z(d):
        k = up(z, d, NZ)
        remote(ps.at[k], pr.at[z], pz_s, pz_r.at[z], dev(k, x, c)).start()

    def right_x(zz):
        ref = rb.at[zz, x, c]
        for way in range(2):
            remote(ref, ref, rx_s.at[way], rx_r.at[way], xdev(1 if way == 0 else -1)).start()

    def right_half(way):
        ref = rb.at[pl.ds(way * (NZ // 2), NZ // 2), up(x, -1 if way == 0 else 1, NX), c]
        return remote(ref, ref, rx_s.at[2 + way], rx_r.at[2 + way], xdev(1 if way == 0 else -1))

    def right_core(xx, i):
        ref = rb.at[:, xx, c]
        return remote(ref, ref, rd_s.at[i], rd_r.at[i], other)

    def left_x(zz, way):
        ref = lb.at[:, zz, x, c]
        return remote(ref, ref, lx_s.at[zz, way], lx_r.at[zz, way], xdev(1 if way == 0 else -1))

    def left_half(zz, way):
        ref = lb.at[way, zz, up(x, -1 if way == 0 else 1, NX), c]
        return remote(ref, ref, lo_s.at[zz, way], lo_r.at[zz, way], xdev(1 if way == 0 else -1))

    def left_core(zz):
        ref = lb.at[:, zz, :, c]
        return remote(ref, ref, ld_s.at[zz], ld_r.at[zz], other)

    def near(d):
        return [up(z, -d, NZ), up(z, d, NZ)]

    def left_send(group):
        for zz in group:
            for way in range(2):
                left_x(zz, way).start()

    def left_pass(group):
        for zz in group:
            for way in range(2):
                left_x(zz, way).wait_recv()
                left_half(zz, way).start()

    def left_share(group):
        for zz in group:
            for way in range(2):
                left_half(zz, way).wait_recv()
            left_core(zz).start()

    own, two, last = [z], near(2), near(3) + [up(z, 4, NZ)]

    for way in range(2):
        left_z(0, way).start()
    left_send(own)
    right_x(z)
    for d in (1, -1, 2, -2, 3, -3, 4):
        right_z(d)

    loads[2].wait()
    loads[3].wait()

    def pack(k, carry):
        cols = pl.ds(pl.multiple_of(k * width, width), width)
        g = gv[:, cols]
        m = BETA_ONE * mv[:, cols] + (1.0 - BETA_ONE) * g
        mv[:, cols] = m
        ps[k, 0:row] = g.astype(BF16)
        ps[k, row : 2 * row] = m.astype(BF16)
        return carry

    lax.fori_loop(0, NZ, pack, 0)
    store_m = pltpu.make_async_copy(mv, mom_o, out_sem.at[0])
    store_m.start()
    pr[z] = ps[z]

    for way in range(2):
        left_z(0, way).wait_recv()
        left_z(1, way).start()
    for d in FILL:
        packed_z(d)
    left_send(near(1))
    left_pass(own)

    wait(right.at[pl.ds(0, 4)], rz_r.at[0])
    for zz in near(1) + near(2):
        right_x(zz)
    wait(right.at[pl.ds(0, 3)], rz_r.at[1])
    for zz in near(3) + [up(z, 4, NZ)]:
        right_x(zz)

    for way in range(2):
        left_z(1, way).wait_recv()
        left_z(2, way).start()
        left_z(3, way).start()
    for d in REST:
        packed_z(d)
    left_send(two)
    left_pass(near(1))
    left_share(own)

    right_core(x, 0).start()
    for way in range(2):
        wait(rb.at[:, x, c], rx_r.at[way])
        right_half(way).start()
        right_core(up(x, -1 if way == 0 else 1, NX), 1 + way).start()

    for way in range(2):
        left_z(2, way).wait_recv()
        left_z(3, way).wait_recv()
    left_send(last)
    left_pass(two)
    left_share(near(1))

    for way in range(2):
        right_half(way).wait_recv()
    right_core(up(x, 2, NX), 3).start()
    for i in range(4):
        right_core(x, i).wait_recv()

    def order(i):
        d = z
        for step, other_d in enumerate(FILL + REST):
            d = jnp.where(i == step + 1, up(z, -other_d, NZ), d)
        return d

    def turn(i, carry):
        zz = order(i)

        @pl.when(i > 0)
        def _():
            wait(pr.at[zz], pz_r.at[zz])

        t = jnp.dot(pr[zz], rb[...].reshape(width, width), preferred_element_type=F32).astype(BF16)
        seg = width // NP
        for q in range(NP):
            tb[zz, q, :, 0:seg] = t[0:row, q * seg : (q + 1) * seg]
            tb[zz, q, :, seg : 2 * seg] = t[row : 2 * row, q * seg : (q + 1) * seg]
        cb[zz, p] = tb[zz, p]

        def send(e, carry):
            q = lax.rem(p + e, NP)
            remote(tb.at[zz, q], cb.at[zz, p], tx_s, tx_r.at[zz], {"fsdp": z * NP + q}).start()
            return carry

        lax.fori_loop(1, NP, send, 0)
        return carry

    lax.fori_loop(0, 3, turn, 0)
    left_pass(last)
    left_share(two)
    lax.fori_loop(3, 5, turn, 0)
    left_share(last)
    lax.fori_loop(5, 8, turn, 0)

    def left_done(zz, carry):
        left_core(zz).wait_recv()
        return carry

    lax.fori_loop(0, NZ, left_done, 0)
    seg = width // NP
    part = width // 4

    def project(i, carry):
        zz = order(i)
        l, q = zz // 4, lax.rem(zz, 4)
        wait(cb.at[zz, pl.ds(0, NP - 1)], tx_r.at[zz])
        turned = cb[zz].reshape(NP * row, 2 * seg)
        for k in range(4):
            at = slice(k * part, (k + 1) * part)
            basis = lb[l, pl.ds(2 * q, 2), :, :, :, at].reshape(NP * row, part)
            ac[l, at] += lax.dot_general(basis, turned, (((0,), (0,)), ((), ())), preferred_element_type=F32)
        return carry

    lax.fori_loop(0, NZ, project, 0)
    loads[4].wait()

    def scale(l):
        def piece(i, carry):
            inside = pl.ds(pl.multiple_of(i * part, part), part)
            rows = pl.ds(pl.multiple_of(l * width + i * part, part), part)
            g, m = ac[l, inside, :seg], ac[l, inside, seg:]
            s = BETA_TWO * sv[rows, :] + (1.0 - BETA_TWO) * g * g
            sv[rows, :] = s
            sc[rows, :] = (m / (jnp.sqrt(s) + EPSILON)).astype(BF16)
            return carry

        lax.fori_loop(0, 4, piece, 0)

    def far(i):
        d = (NZ - i) // 2
        return up(z, jnp.where(lax.rem(i, 2) == 1, d, -d), NZ)

    def back(i, carry):
        zz = far(i)
        l, q = zz // 4, lax.rem(zz, 4)
        basis = lb[l, pl.ds(2 * q, 2)].reshape(NP * row, width)
        scaled = sc[pl.ds(pl.multiple_of(l * width, width), width), :]
        out = jnp.dot(basis, scaled, preferred_element_type=F32).astype(BF16)
        bk[zz] = out.reshape(NP, row, seg)
        wb[zz, p] = bk[zz, p]

        def send(e, carry):
            q = lax.rem(p + e, NP)
            remote(bk.at[zz, q], wb.at[zz, p], bx_s, bx_r.at[zz], {"fsdp": z * NP + q}).start()
            return carry

        lax.fori_loop(1, NP, send, 0)
        return carry

    first = up(z, 4, NZ) // 4
    scale(first)
    lax.fori_loop(0, 1, back, 0)
    scale(1 - first)
    store_s = pltpu.make_async_copy(sv, sec_o, out_sem.at[1])
    store_s.start()
    lax.fori_loop(1, NZ, back, 0)

    mine = pl.ds(pl.multiple_of(z * width, width), width)

    def update(i, carry):
        zz = far(i)
        wait(wb.at[zz, pl.ds(0, NP - 1)], bx_r.at[zz])
        rows = jnp.concatenate([wb[zz, q] for q in range(NP)], axis=1)
        out = lax.dot_general(
            rows, rb[...].reshape(width, width), (((1,), (1,)), ((), ())), preferred_element_type=F32
        )
        ub[zz] = out.astype(BF16)

        @pl.when(i < NZ - 1)
        def _():
            remote(ub.at[zz], upd_o.at[:, mine], uz_s, uz_r, dev(zz, x, c)).start()

        return carry

    lax.fori_loop(0, NZ, update, 0)
    store_u = pltpu.make_async_copy(ub.at[z], upd_o.at[:, mine], out_sem.at[2])
    store_u.start()

    for way in range(2):
        wait(rb.at[:, x, c], rx_s.at[way])
        right_half(way).wait_send()
        for step in range(4):
            left_z(step, way).wait_send()
    for i in range(4):
        right_core(x, i).wait_send()

    def drain(zz, carry):
        for way in range(2):
            left_x(zz, way).wait_send()
            left_half(zz, way).wait_send()
        left_core(zz).wait_send()
        return carry

    lax.fori_loop(0, NZ, drain, 0)
    wait(right.at[pl.ds(0, NZ - 1)], rz_s)
    wait(ps.at[pl.ds(0, NZ - 1)], pz_s)
    wait(tb.at[pl.ds(0, NZ - 1)], tx_s)
    wait(bk.at[pl.ds(0, NZ - 1)], bx_s)
    wait(ub.at[pl.ds(0, NZ - 1)], uz_s)
    wait(ub.at[pl.ds(0, NZ - 1)], uz_r)
    store_m.wait()
    store_s.wait()
    store_u.wait()


def finish(update, mom, sec, upd_o, mom_o, sec_o, ub, uf, mb, sb, sem):
    parts = 4
    step = uf.shape[1] // parts
    cols = [pl.ds(i * step, step) for i in range(parts)]
    loads = [pltpu.make_async_copy(update.at[:, at], ub.at[:, at], sem.at[i]) for i, at in enumerate(cols)]
    loads += [pltpu.make_async_copy(mom, mb, sem.at[parts]), pltpu.make_async_copy(sec, sb, sem.at[parts + 1])]
    for load in loads:
        load.start()
    stores = []
    for i, at in enumerate(cols):
        loads[i].wait()
        uf[:, at] = ub[:, at].astype(F32)
        stores.append(pltpu.make_async_copy(uf.at[:, at], upd_o.at[:, at], sem.at[parts + 2 + i]))
        stores[-1].start()
    for i, (held, out) in enumerate(((mb, mom_o), (sb, sec_o))):
        loads[parts + i].wait()
        stores.append(pltpu.make_async_copy(held, out, sem.at[2 * parts + 2 + i]))
        stores[-1].start()
    for store in stores:
        store.wait()


def local(grad, moment, second, left_basis, right_basis):
    row, cols = grad.shape
    lblocks, piece, width = left_basis.shape
    total, seg = second.shape
    any_spec = pl.BlockSpec(memory_space=pl.ANY)
    dma = pltpu.SemaphoreType.DMA
    update, moment_new, second_new = pl.pallas_call(
        kernel,
        out_shape=(
            jax.ShapeDtypeStruct((row, cols), BF16),
            jax.ShapeDtypeStruct((row, cols), F32),
            jax.ShapeDtypeStruct((total, seg), F32),
        ),
        in_specs=[any_spec] * 5,
        out_specs=[any_spec] * 3,
        scratch_shapes=[
            pltpu.VMEM((row, cols), F32),
            pltpu.VMEM((row, cols), F32),
            pltpu.VMEM((total, seg), F32),
            pltpu.VMEM((NZ, 2 * row, width), BF16),
            pltpu.VMEM((NZ, 2 * row, width), BF16),
            pltpu.VMEM((NZ, NX, NC, piece, width), BF16),
            pltpu.VMEM((NZ, NP, row, 2 * seg), BF16),
            pltpu.VMEM((NZ, NP, row, 2 * seg), BF16),
            pltpu.VMEM((lblocks, NZ, NX, NC, piece, width), BF16),
            pltpu.VMEM((lblocks, width, 2 * seg), F32),
            pltpu.VMEM((total, seg), BF16),
            pltpu.VMEM((NZ, NP, row, seg), BF16),
            pltpu.VMEM((NZ, NP, row, seg), BF16),
            pltpu.VMEM((NZ, row, width), BF16),
            dma((5,)), dma((3,)),
            dma, dma((2,)), dma((4,)), dma((4,)), dma((4,)), dma((4,)),
            dma((4, 2)), dma((4, 2)), dma((NZ, 2)), dma((NZ, 2)), dma((NZ, 2)), dma((NZ, 2)), dma((NZ,)), dma((NZ,)),
            dma, dma((NZ,)), dma, dma((NZ,)), dma, dma((NZ,)), dma, dma,
        ],
        compiler_params=pltpu.CompilerParams(
            collective_id=0, has_side_effects=True, vmem_limit_bytes=62 * 2**20
        ),
        cost_estimate=pl.CostEstimate(flops=3 * 2**30, bytes_accessed=8 * 2**20, transcendentals=2**19),
        name="soap_step",
    )(grad, moment, second, left_basis, right_basis)
    return pl.pallas_call(
        finish,
        out_shape=(
            jax.ShapeDtypeStruct((row, cols), F32),
            jax.ShapeDtypeStruct((row, cols), F32),
            jax.ShapeDtypeStruct((total, seg), F32),
        ),
        in_specs=[any_spec] * 3,
        out_specs=[pl.BlockSpec(memory_space=pltpu.MemorySpace.HBM)] * 3,
        scratch_shapes=[pltpu.VMEM((row, cols), BF16), pltpu.VMEM((row, cols), F32), pltpu.VMEM((row, cols), F32), pltpu.VMEM((total, seg), F32), dma((12,))],
        compiler_params=pltpu.CompilerParams(vmem_limit_bytes=62 * 2**20),
        name="finish",
    )(update, moment_new, second_new)


def solution(mesh):
    in_specs = (
        P(("dp", "fsdp"), None),
        P(("dp", "fsdp"), None),
        P("dp", "fsdp"),
        P("dp", "fsdp", None),
        P("dp", "fsdp", None),
    )
    out_specs = (P(("dp", "fsdp"), None), P(("dp", "fsdp"), None), P("dp", "fsdp"))
    return jax.shard_map(local, mesh=mesh, in_specs=in_specs, out_specs=out_specs, check_vma=False)
```

time: 82.4 us -> 75.6 us (0.917)
  local copies, waits for them, and re-layouts: 2.58 us -> 0 us
  other arithmetic: 2.17 us -> 0 us
  Pallas kernels: 76.8 us -> 74.8 us
    pallas_call x1, Pallas kernels: 76.8 us -> 71.9 us  [local(): pl.pallas_call(kernel, out_shape=(jax.ShapeDtypeStruct((row, cols), BF16)...]
    pallas_call x0 -> x1, Pallas kernels: none -> 2.92 us  [local(): pl.pallas_call(finish, out_shape=(jax.ShapeDtypeStruct((row, cols), F32),...]
    unnamed x6 -> x0, local copies, waits for them, and re-layouts: 2.58 us -> none
    convert_element_type x1 -> x0, other arithmetic: 2.17 us -> none  [local(): return (update.astype(F32), moment_new, second_new)]
where the time goes in v3:
time: 75.6 us; the launch traced here: 75.5 us
  Pallas kernels  74.8 us (99%)
    pallas_call x1, Pallas kernels, local(): pl.pallas_call(kernel, out_shape=(jax.ShapeDtypeStruct((row, cols), BF16)...  71.9 us
    pallas_call x1, Pallas kernels, local(): pl.pallas_call(finish, out_shape=(jax.ShapeDtypeStruct((row, cols), F32),...  2.92 us

profile of v3, /device:TPU:1, one launch (start us, length us, event | category | flops | bytes accessed | tf_op | source)
XLA Modules:
  0.0 75.5 jit_solution(6028316521566922285)
XLA Ops:
  0.6 71.9 %soap_step.1 = (bf16[32,8192]{1,0:T(8,128)(2,1)}, f32[32,8192]{1,0:T(8,128)}, f32[2048,128]{1,0:T(8,128)}) custom-call(f32[32,8192]{1,0:T(8,128)} %grad.1, f32[32,8192]{1,0:T(8,128)} %moment.1, f32[2048,128]{1,0:T(8,128)} %second.1, bf16[2,16,1024]{2,1,0:T(8,128)(2,1)} %left.1, bf16[8,16,1024]{2,1,0:T(8,128)(2,1)} %right.1), custom_call_target="tpu_custom_call" | custom-call | flops 3221225472 | bytes 8388608 | tf_op jit(solution)/shard_map/soap_step/pallas_call | solution.py:381
  72.5 2.9 %finish.1 = (f32[32,8192]{1,0:T(8,128)}, f32[32,8192]{1,0:T(8,128)}, f32[2048,128]{1,0:T(8,128)}) custom-call(bf16[32,8192]{1,0:T(8,128)(2,1)} %get-tuple-element.6.update, f32[32,8192]{1,0:T(8,128)} %get-tuple-element.7.mom, f32[2048,128]{1,0:T(8,128)} %get-tuple-element.8.sec), custom_call_target="tpu_custom_call" | custom-call | tf_op jit(solution)/shard_map/finish/pallas_call | solution.py:416

commit v4 on v3

--- a/solution.py
+++ b/solution.py
@@ -15,6 +15,9 @@
 
 FILL = (1, -1)
 REST = (2, -2, 3, -3, 4)
+LAST = REST[-1]
+
+RETURN = (3, -3, 2, -2, 4, 1, -1)
 
 
 def kernel(
@@ -24,7 +27,7 @@
     in_sem, out_sem,
     rz_s, rz_r, rx_s, rx_r, rd_s, rd_r,
     lz_s, lz_r, lx_s, lx_r, lo_s, lo_r, ld_s, ld_r,
-    pz_s, pz_r, tx_s, tx_r, bx_s, bx_r, uz_s, uz_r,
+    pz_s, pz_r, pl_r, tx_s, tx_r, bx_s, bx_r, uz_s, uz_r,
 ):
     f = lax.axis_index("fsdp")
     z, p = f // NP, lax.rem(f, NP)
@@ -87,7 +90,12 @@
 
     def packed_z(d):
         k = up(z, d, NZ)
-        remote(ps.at[k], pr.at[z], pz_s, pz_r.at[z], dev(k, x, c)).start()
+        if d != LAST:
+            remote(ps.at[k], pr.at[z], pz_s, pz_r.at[z], dev(k, x, c)).start()
+            return
+        for h in range(2):
+            rows = pl.ds(h * (row // 2), row // 2)
+            remote(ps.at[k, :, rows], pr.at[z, :, rows], pz_s, pl_r.at[h], dev(k, x, c)).start()
 
     def right_x(zz):
         ref = rb.at[zz, x, c]
@@ -116,6 +124,10 @@
 
     def near(d):
         return [up(z, -d, NZ), up(z, d, NZ)]
+
+    def left_opposite(way):
+        ref = lb.at[way, z, x, c]
+        return remote(ref, ref, lo_s.at[z, way], lo_r.at[z, way], xdev(2))
 
     def left_send(group):
         for zz in group:
@@ -140,6 +152,8 @@
         left_z(0, way).start()
     left_send(own)
     right_x(z)
+    for way in range(2):
+        left_opposite(way).start()
     for d in (1, -1, 2, -2, 3, -3, 4):
         right_z(d)
 
@@ -151,8 +165,8 @@
         g = gv[:, cols]
         m = BETA_ONE * mv[:, cols] + (1.0 - BETA_ONE) * g
         mv[:, cols] = m
-        ps[k, 0:row] = g.astype(BF16)
-        ps[k, row : 2 * row] = m.astype(BF16)
+        ps[k, 0] = g.astype(BF16)
+        ps[k, 1] = m.astype(BF16)
         return carry
 
     lax.fori_loop(0, NZ, pack, 0)
@@ -166,11 +180,11 @@
     for d in FILL:
         packed_z(d)
     left_send(near(1))
-    left_pass(own)
 
     wait(right.at[pl.ds(0, 4)], rz_r.at[0])
     for zz in near(1) + near(2):
         right_x(zz)
+    left_pass(near(1))
     wait(right.at[pl.ds(0, 3)], rz_r.at[1])
     for zz in near(3) + [up(z, 4, NZ)]:
         right_x(zz)
@@ -182,7 +196,8 @@
     for d in REST:
         packed_z(d)
     left_send(two)
-    left_pass(near(1))
+    for way in range(2):
+        left_x(z, way).wait_recv()
     left_share(own)
 
     right_core(x, 0).start()
@@ -193,10 +208,12 @@
 
     for way in range(2):
         left_z(2, way).wait_recv()
-        left_z(3, way).wait_recv()
-    left_send(last)
+    left_send(near(3))
     left_pass(two)
     left_share(near(1))
+    for way in range(2):
+        left_z(3, way).wait_recv()
+    left_send([up(z, 4, NZ)])
 
     for way in range(2):
         right_half(way).wait_recv()
@@ -210,6 +227,23 @@
             d = jnp.where(i == step + 1, up(z, -other_d, NZ), d)
         return d
 
+    def turn_rows(zz, h0, rows):
+        at = pl.ds(h0, rows)
+        both = pr[zz, :, at].reshape(2 * rows, width)
+        t = jnp.dot(both, rb[...].reshape(width, width), preferred_element_type=F32).astype(BF16)
+        seg = width // NP
+        for q in range(NP):
+            tb[zz, q, at, 0:seg] = t[0:rows, q * seg : (q + 1) * seg]
+            tb[zz, q, at, seg : 2 * seg] = t[rows : 2 * rows, q * seg : (q + 1) * seg]
+        cb[zz, p, at] = tb[zz, p, at]
+
+        def send(e, carry):
+            q = lax.rem(p + e, NP)
+            remote(tb.at[zz, q, at], cb.at[zz, p, at], tx_s, tx_r.at[zz], {"fsdp": z * NP + q}).start()
+            return carry
+
+        lax.fori_loop(1, NP, send, 0)
+
     def turn(i, carry):
         zz = order(i)
 
@@ -217,19 +251,13 @@
         def _():
             wait(pr.at[zz], pz_r.at[zz])
 
-        t = jnp.dot(pr[zz], rb[...].reshape(width, width), preferred_element_type=F32).astype(BF16)
-        seg = width // NP
-        for q in range(NP):
-            tb[zz, q, :, 0:seg] = t[0:row, q * seg : (q + 1) * seg]
-            tb[zz, q, :, seg : 2 * seg] = t[row : 2 * row, q * seg : (q + 1) * seg]
-        cb[zz, p] = tb[zz, p]
-
-        def send(e, carry):
-            q = lax.rem(p + e, NP)
-            remote(tb.at[zz, q], cb.at[zz, p], tx_s, tx_r.at[zz], {"fsdp": z * NP + q}).start()
-            return carry
-
-        lax.fori_loop(1, NP, send, 0)
+        turn_rows(zz, 0, row)
+        return carry
+
+    def turn_last(h, carry):
+        half = row // 2
+        wait(pr.at[0, :, pl.ds(0, half)], pl_r.at[h])
+        turn_rows(up(z, -LAST, NZ), pl.multiple_of(h * half, half), half)
         return carry
 
     lax.fori_loop(0, 3, turn, 0)
@@ -237,7 +265,8 @@
     left_share(two)
     lax.fori_loop(3, 5, turn, 0)
     left_share(last)
-    lax.fori_loop(5, 8, turn, 0)
+    lax.fori_loop(5, 7, turn, 0)
+    lax.fori_loop(0, 2, turn_last, 0)
 
     def left_done(zz, carry):
         left_core(zz).wait_recv()
@@ -274,8 +303,10 @@
         lax.fori_loop(0, 4, piece, 0)
 
     def far(i):
-        d = (NZ - i) // 2
-        return up(z, jnp.where(lax.rem(i, 2) == 1, d, -d), NZ)
+        zz = z
+        for step, d in enumerate(RETURN):
+            zz = jnp.where(i == step, up(z, d, NZ), zz)
+        return zz
 
     def back(i, carry):
         zz = far(i)
@@ -294,7 +325,7 @@
         lax.fori_loop(1, NP, send, 0)
         return carry
 
-    first = up(z, 4, NZ) // 4
+    first = up(z, RETURN[0], NZ) // 4
     scale(first)
     lax.fori_loop(0, 1, back, 0)
     scale(1 - first)
@@ -350,23 +381,18 @@
     store_u.wait()
 
 
-def finish(update, mom, sec, upd_o, mom_o, sec_o, ub, uf, mb, sb, sem):
+def finish(update, mom, sec, upd_o, mom_o, sec_o, ub, uf, sem):
     parts = 4
     step = uf.shape[1] // parts
     cols = [pl.ds(i * step, step) for i in range(parts)]
     loads = [pltpu.make_async_copy(update.at[:, at], ub.at[:, at], sem.at[i]) for i, at in enumerate(cols)]
-    loads += [pltpu.make_async_copy(mom, mb, sem.at[parts]), pltpu.make_async_copy(sec, sb, sem.at[parts + 1])]
-    for load in loads:
-        load.start()
-    stores = []
+    stores = [pltpu.make_async_copy(mom, mom_o, sem.at[parts]), pltpu.make_async_copy(sec, sec_o, sem.at[parts + 1])]
+    for copy in loads + stores:
+        copy.start()
     for i, at in enumerate(cols):
         loads[i].wait()
         uf[:, at] = ub[:, at].astype(F32)
         stores.append(pltpu.make_async_copy(uf.at[:, at], upd_o.at[:, at], sem.at[parts + 2 + i]))
-        stores[-1].start()
-    for i, (held, out) in enumerate(((mb, mom_o), (sb, sec_o))):
-        loads[parts + i].wait()
-        stores.append(pltpu.make_async_copy(held, out, sem.at[2 * parts + 2 + i]))
         stores[-1].start()
     for store in stores:
         store.wait()
@@ -380,19 +406,15 @@
     dma = pltpu.SemaphoreType.DMA
     update, moment_new, second_new = pl.pallas_call(
         kernel,
-        out_shape=(
-            jax.ShapeDtypeStruct((row, cols), BF16),
-            jax.ShapeDtypeStruct((row, cols), F32),
-            jax.ShapeDtypeStruct((total, seg), F32),
-        ),
+        out_shape=(pltpu.VMEM((row, cols), BF16), pltpu.VMEM((row, cols), F32), pltpu.VMEM((total, seg), F32)),
         in_specs=[any_spec] * 5,
         out_specs=[any_spec] * 3,
         scratch_shapes=[
             pltpu.VMEM((row, cols), F32),
             pltpu.VMEM((row, cols), F32),
             pltpu.VMEM((total, seg), F32),
-            pltpu.VMEM((NZ, 2 * row, width), BF16),
-            pltpu.VMEM((NZ, 2 * row, width), BF16),
+            pltpu.VMEM((NZ, 2, row, width), BF16),
+            pltpu.VMEM((NZ, 2, row, width), BF16),
             pltpu.VMEM((NZ, NX, NC, piece, width), BF16),
             pltpu.VMEM((NZ, NP, row, 2 * seg), BF16),
             pltpu.VMEM((NZ, NP, row, 2 * seg), BF16),
@@ -405,10 +427,10 @@
             dma((5,)), dma((3,)),
             dma, dma((2,)), dma((4,)), dma((4,)), dma((4,)), dma((4,)),
             dma((4, 2)), dma((4, 2)), dma((NZ, 2)), dma((NZ, 2)), dma((NZ, 2)), dma((NZ, 2)), dma((NZ,)), dma((NZ,)),
-            dma, dma((NZ,)), dma, dma((NZ,)), dma, dma((NZ,)), dma, dma,
+            dma, dma((NZ,)), dma((2,)), dma, dma((NZ,)), dma, dma((NZ,)), dma, dma,
         ],
         compiler_params=pltpu.CompilerParams(
-            collective_id=0, has_side_effects=True, vmem_limit_bytes=62 * 2**20
+            collective_id=0, has_side_effects=True, vmem_limit_bytes=61 * 2**20 + 2**18
         ),
         cost_estimate=pl.CostEstimate(flops=3 * 2**30, bytes_accessed=8 * 2**20, transcendentals=2**19),
         name="soap_step",
@@ -422,8 +444,8 @@
         ),
         in_specs=[any_spec] * 3,
         out_specs=[pl.BlockSpec(memory_space=pltpu.MemorySpace.HBM)] * 3,
-        scratch_shapes=[pltpu.VMEM((row, cols), BF16), pltpu.VMEM((row, cols), F32), pltpu.VMEM((row, cols), F32), pltpu.VMEM((total, seg), F32), dma((12,))],
-        compiler_params=pltpu.CompilerParams(vmem_limit_bytes=62 * 2**20),
+        scratch_shapes=[pltpu.VMEM((row, cols), BF16), pltpu.VMEM((row, cols), F32), dma((10,))],
+        compiler_params=pltpu.CompilerParams(vmem_limit_bytes=16 * 2**20),
         name="finish",
     )(update, moment_new, second_new)
 

time: 75.6 us -> 73.4 us (0.971)
  Pallas kernels: 74.8 us -> 72.7 us
    pallas_call x1, Pallas kernels: 71.9 us -> 70.7 us  [local(): pl.pallas_call(kernel, out_shape=(pltpu.VMEM((row, cols), BF16), pltpu.VM...]
    pallas_call x1, Pallas kernels: 2.92 us -> 1.91 us  [local(): pl.pallas_call(finish, out_shape=(jax.ShapeDtypeStruct((row, cols), F32),...]
where the time goes in v4:
time: 73.4 us; the launch traced here: 73.3 us
  Pallas kernels  72.7 us (99%)
    pallas_call x1, Pallas kernels, local(): pl.pallas_call(kernel, out_shape=(pltpu.VMEM((row, cols), BF16), pltpu.VM...  70.7 us
    pallas_call x1, Pallas kernels, local(): pl.pallas_call(finish, out_shape=(jax.ShapeDtypeStruct((row, cols), F32),...  1.91 us

profile of v4, /device:TPU:1, one launch (start us, length us, event | category | flops | bytes accessed | tf_op | source)
XLA Modules:
  0.0 73.3 jit_solution(7704984910973286813)
XLA Ops:
  0.6 70.7 %soap_step.1 = (bf16[32,8192]{1,0:T(8,128)(2,1)S(1)}, f32[32,8192]{1,0:T(8,128)S(1)}, f32[2048,128]{1,0:T(8,128)S(1)}) custom-call(f32[32,8192]{1,0:T(8,128)} %grad.1, f32[32,8192]{1,0:T(8,128)} %moment.1, f32[2048,128]{1,0:T(8,128)} %second.1, bf16[2,16,1024]{2,1,0:T(8,128)(2,1)} %left.1, bf16[8,16,1024]{2,1,0:T(8,128)(2,1)} %right.1), custom_call_target="tpu_custom_call" | custom-call | flops 3221225472 | bytes 8388608 | tf_op jit(solution)/shard_map/soap_step/pallas_call | solution.py:407
  71.4 1.9 %finish.1 = (f32[32,8192]{1,0:T(8,128)}, f32[32,8192]{1,0:T(8,128)}, f32[2048,128]{1,0:T(8,128)}) custom-call(bf16[32,8192]{1,0:T(8,128)(2,1)S(1)} %get-tuple-element.6.update, f32[32,8192]{1,0:T(8,128)S(1)} %get-tuple-element.7.mom, f32[2048,128]{1,0:T(8,128)S(1)} %get-tuple-element.8.sec), custom_call_target="tpu_custom_call" | custom-call | tf_op jit(solution)/shard_map/finish/pallas_call | solution.py:438

commit v5 on v4

--- a/solution.py
+++ b/solution.py
@@ -23,8 +23,8 @@
 def kernel(
     grad, moment, second, left, right,
     upd_o, mom_o, sec_o,
-    gv, mv, sv, ps, pr, rb, tb, cb, lb, ac, sc, bk, wb, ub,
-    in_sem, out_sem,
+    gv, mv, sv, ps, pr, rb, rt, tb, cb, lb, ac, sc, bk, wb, ub,
+    here, in_sem, out_sem,
     rz_s, rz_r, rx_s, rx_r, rd_s, rd_r,
     lz_s, lz_r, lx_s, lx_r, lo_s, lo_r, ld_s, ld_r,
     pz_s, pz_r, pl_r, tx_s, tx_r, bx_s, bx_r, uz_s, uz_r,
@@ -58,7 +58,7 @@
         pltpu.make_async_copy(ref, ref, sem).wait()
 
     barrier = pltpu.get_barrier_semaphore()
-    for d in (4, 3, -3, 2, -2, 1, -1):
+    for d in (1, -1):
         pl.semaphore_signal(barrier, inc=1, device_id=zdev(d), device_id_type=pl.DeviceIdType.MESH)
     for d in range(1, NP):
         to = {"fsdp": z * NP + lax.rem(p + d, NP)}
@@ -76,7 +76,7 @@
     ac[...] = jnp.zeros_like(ac)
     loads[0].wait()
     loads[1].wait()
-    pl.semaphore_wait(barrier, 2 * (NZ - 1))
+    pl.semaphore_wait(barrier, 2 + NP - 1)
 
     def right_z(d):
         group = 0 if abs(d) <= 2 else 1
@@ -154,8 +154,18 @@
     right_x(z)
     for way in range(2):
         left_opposite(way).start()
-    for d in (1, -1, 2, -2, 3, -3, 4):
+    for d in (1, -1):
         right_z(d)
+
+    for s in range(1, NZ // 2):
+        ways = range(2) if s < NZ // 2 - 1 else range(1)
+        for way in ways:
+            to = zdev(1 if way == 0 else -1)
+            pl.semaphore_signal(here.at[s - 1, way], inc=1, device_id=to, device_id_type=pl.DeviceIdType.MESH)
+        for way in ways:
+            pl.semaphore_wait(here.at[s - 1, way], 1)
+        for way in ways:
+            right_z(s + 1 if way == 0 else -s - 1)
 
     loads[2].wait()
     loads[3].wait()
@@ -264,6 +274,15 @@
     left_pass(last)
     left_share(two)
     lax.fori_loop(3, 5, turn, 0)
+
+    def transpose(i, carry):
+        planes = pl.ds(i * 2, 2)
+        rt[:, pl.ds(pl.multiple_of(i * 2 * NP * rb.shape[3], 2 * NP * rb.shape[3]), 2 * NP * rb.shape[3])] = (
+            rb[planes].reshape(2 * NP * rb.shape[3], width).T
+        )
+        return carry
+
+    lax.fori_loop(0, NZ // 2, transpose, 0)
     left_share(last)
     lax.fori_loop(5, 7, turn, 0)
     lax.fori_loop(0, 2, turn_last, 0)
@@ -339,9 +358,7 @@
         zz = far(i)
         wait(wb.at[zz, pl.ds(0, NP - 1)], bx_r.at[zz])
         rows = jnp.concatenate([wb[zz, q] for q in range(NP)], axis=1)
-        out = lax.dot_general(
-            rows, rb[...].reshape(width, width), (((1,), (1,)), ((), ())), preferred_element_type=F32
-        )
+        out = jnp.dot(rows, rt[...], preferred_element_type=F32)
         ub[zz] = out.astype(BF16)
 
         @pl.when(i < NZ - 1)
@@ -416,6 +433,7 @@
             pltpu.VMEM((NZ, 2, row, width), BF16),
             pltpu.VMEM((NZ, 2, row, width), BF16),
             pltpu.VMEM((NZ, NX, NC, piece, width), BF16),
+            pltpu.VMEM((width, width), BF16),
             pltpu.VMEM((NZ, NP, row, 2 * seg), BF16),
             pltpu.VMEM((NZ, NP, row, 2 * seg), BF16),
             pltpu.VMEM((lblocks, NZ, NX, NC, piece, width), BF16),
@@ -424,7 +442,7 @@
             pltpu.VMEM((NZ, NP, row, seg), BF16),
             pltpu.VMEM((NZ, NP, row, seg), BF16),
             pltpu.VMEM((NZ, row, width), BF16),
-            dma((5,)), dma((3,)),
+            pltpu.SemaphoreType.REGULAR((NZ // 2 - 1, 2)), dma((5,)), dma((3,)),
             dma, dma((2,)), dma((4,)), dma((4,)), dma((4,)), dma((4,)),
             dma((4, 2)), dma((4, 2)), dma((NZ, 2)), dma((NZ, 2)), dma((NZ, 2)), dma((NZ, 2)), dma((NZ,)), dma((NZ,)),
             dma, dma((NZ,)), dma((2,)), dma, dma((NZ,)), dma, dma((NZ,)), dma, dma,

time: 73.4 us -> 72.8 us (level)
  no operation moved by 1% of the time
where the time goes in v5:
time: 72.8 us; the launch traced here: 72.7 us
  Pallas kernels  72.1 us (99%)
    pallas_call x1, Pallas kernels, local(): pl.pallas_call(kernel, out_shape=(pltpu.VMEM((row, cols), BF16), pltpu.VM...  70.2 us
    pallas_call x1, Pallas kernels, local(): pl.pallas_call(finish, out_shape=(jax.ShapeDtypeStruct((row, cols), F32),...  1.91 us

profile of v5, /device:TPU:1, one launch (start us, length us, event | category | flops | bytes accessed | tf_op | source)
XLA Modules:
  0.0 72.7 jit_solution(12197784888488515901)
XLA Ops:
  0.6 70.2 %soap_step.1 = (bf16[32,8192]{1,0:T(8,128)(2,1)S(1)}, f32[32,8192]{1,0:T(8,128)S(1)}, f32[2048,128]{1,0:T(8,128)S(1)}) custom-call(f32[32,8192]{1,0:T(8,128)} %grad.1, f32[32,8192]{1,0:T(8,128)} %moment.1, f32[2048,128]{1,0:T(8,128)} %second.1, bf16[2,16,1024]{2,1,0:T(8,128)(2,1)} %left.1, bf16[8,16,1024]{2,1,0:T(8,128)(2,1)} %right.1), custom_call_target="tpu_custom_call" | custom-call | flops 3221225472 | bytes 8388608 | tf_op jit(solution)/shard_map/soap_step/pallas_call | solution.py:424
  70.8 1.9 %finish.1 = (f32[32,8192]{1,0:T(8,128)}, f32[32,8192]{1,0:T(8,128)}, f32[2048,128]{1,0:T(8,128)}) custom-call(bf16[32,8192]{1,0:T(8,128)(2,1)S(1)} %get-tuple-element.6.update, f32[32,8192]{1,0:T(8,128)S(1)} %get-tuple-element.7.mom, f32[2048,128]{1,0:T(8,128)S(1)} %get-tuple-element.8.sec), custom_call_target="tpu_custom_call" | custom-call | tf_op jit(solution)/shard_map/finish/pallas_call | solution.py:456

commit v6 on v5

--- a/solution.py
+++ b/solution.py
@@ -248,7 +248,7 @@
         cb[zz, p, at] = tb[zz, p, at]
 
         def send(e, carry):
-            q = lax.rem(p + e, NP)
+            q = lax.rem(p + 1 + lax.rem(e + 2, NP - 1), NP)
             remote(tb.at[zz, q, at], cb.at[zz, p, at], tx_s, tx_r.at[zz], {"fsdp": z * NP + q}).start()
             return carry
 
@@ -337,7 +337,7 @@
         wb[zz, p] = bk[zz, p]
 
         def send(e, carry):
-            q = lax.rem(p + e, NP)
+            q = lax.rem(p + 1 + lax.rem(e + 2, NP - 1), NP)
             remote(bk.at[zz, q], wb.at[zz, p], bx_s, bx_r.at[zz], {"fsdp": z * NP + q}).start()
             return carry
 

time: 72.8 us -> 72.8 us (level)
  no operation moved by 1% of the time
where the time goes in v6:
time: 72.8 us
  Pallas kernels  72.1 us (99%)
    pallas_call x1, Pallas kernels, local(): pl.pallas_call(kernel, out_shape=(pltpu.VMEM((row, cols), BF16), pltpu.VM...  70.2 us
    pallas_call x1, Pallas kernels, local(): pl.pallas_call(finish, out_shape=(jax.ShapeDtypeStruct((row, cols), F32),...  1.91 us

profile of v6, /device:TPU:1, one launch (start us, length us, event | category | flops | bytes accessed | tf_op | source)
XLA Modules:
  0.0 72.8 jit_solution(13472556100759724537)
XLA Ops:
  0.6 70.2 %soap_step.1 = (bf16[32,8192]{1,0:T(8,128)(2,1)S(1)}, f32[32,8192]{1,0:T(8,128)S(1)}, f32[2048,128]{1,0:T(8,128)S(1)}) custom-call(f32[32,8192]{1,0:T(8,128)} %grad.1, f32[32,8192]{1,0:T(8,128)} %moment.1, f32[2048,128]{1,0:T(8,128)} %second.1, bf16[2,16,1024]{2,1,0:T(8,128)(2,1)} %left.1, bf16[8,16,1024]{2,1,0:T(8,128)(2,1)} %right.1), custom_call_target="tpu_custom_call" | custom-call | flops 3221225472 | bytes 8388608 | tf_op jit(solution)/shard_map/soap_step/pallas_call | solution.py:424
  70.9 1.9 %finish.1 = (f32[32,8192]{1,0:T(8,128)}, f32[32,8192]{1,0:T(8,128)}, f32[2048,128]{1,0:T(8,128)}) custom-call(bf16[32,8192]{1,0:T(8,128)(2,1)S(1)} %get-tuple-element.6.update, f32[32,8192]{1,0:T(8,128)S(1)} %get-tuple-element.7.mom, f32[2048,128]{1,0:T(8,128)S(1)} %get-tuple-element.8.sec), custom_call_target="tpu_custom_call" | custom-call | tf_op jit(solution)/shard_map/finish/pallas_call | solution.py:456
